TPU v7x, 256 devices: a whole 4x4x8 slice. The times are simulated.
256 devices in a mesh: view: 8 (over x, z_lo), gz: 32 (over y, z_hi, core).
Axes of the slice: x: 4, y: 4, z: 8 (z_hi: 4, z_lo: 2; z = z_hi * 2 + z_lo), core: 2. Of those that a mesh axis runs over, the one named last changes fastest.
Arguments:
- views_data: bfloat16 [8, 1024, 128, 256], P('view', 'gz'), may hold values from 0.29882812 to 3
- psf: float32 [8, 3, 31], P('view'), may hold values from 0.02 to 1
- start: float32 [1024, 128, 256], P('gz'), may hold values from 0.05 to 12, as said below
Outputs:
- estimate: float32 [1024, 128, 256], P('gz')
Inputs may be any that keep to these rules, and one draw needn't show every extreme that they name: `start`: positive.
All inputs are finite; a program needn't handle non-finite values.
Results may differ from a plain program's by a relative error of at most 0.0003.
Values may be sent and summed in bfloat16 or wider, within the bound.
No kernel may reach another device: no remote copies, remote signals or barrier semaphores. Data moves between devices by JAX's collectives and lax.ppermute only.
A program may use at most 128 MiB of HBM per device.

v0:
```python
import jax
import jax.numpy as jnp
from jax import lax
from jax.sharding import PartitionSpec as P

RADIUS = 15
TAPS = 31
ITERS = 2


def with_halo(block, sides, width):
    for axis, dim in sides:
        count = lax.axis_size(axis)
        forward = [(i, i + 1) for i in range(count - 1)]
        backward = [(target, source) for source, target in forward]
        low = lax.ppermute(
            lax.slice_in_dim(block, block.shape[dim] - width, None, axis=dim), axis, forward
        )
        high = lax.ppermute(lax.slice_in_dim(block, 0, width, axis=dim), axis, backward)
        block = jnp.concatenate([low, block, high], axis=dim)
    return block


def band_matrix(kernel_row, n_out, n_in, offset, direction):
    out_index = jnp.arange(n_out, dtype=jnp.int32)[:, None]
    in_index = jnp.arange(n_in, dtype=jnp.int32)[None, :]
    tap_index = direction * (in_index - out_index - offset) + RADIUS
    one_hot = (tap_index[:, :, None] == jnp.arange(TAPS, dtype=jnp.int32)[None, None, :]).astype(
        jnp.float32
    )
    return jnp.sum(one_hot * kernel_row[None, None, :], axis=2)


def apply_planes(volume, matrix_x, matrix_y):
    volume = jnp.einsum("zxy,ox->zoy", volume, matrix_x, precision=lax.Precision.HIGHEST)
    return jnp.einsum("zxy,oy->zxo", volume, matrix_y, precision=lax.Precision.HIGHEST)


def apply_depth(volume, matrix_z):
    return jnp.einsum("zxy,oz->oxy", volume, matrix_z, precision=lax.Precision.HIGHEST)


def per_device(views_data, psf, start):
    kernels = psf[0] / jnp.sum(psf[0], axis=1, keepdims=True)
    recorded = views_data[0]
    depth_cz, width_x, width_y = recorded.shape
    view_count = lax.axis_size("view")
    forward_x = band_matrix(kernels[0], width_x, width_x, 0, 1)
    forward_y = band_matrix(kernels[1], width_y, width_y, 0, 1)
    adjoint_x = band_matrix(kernels[0], width_x, width_x, 0, -1)
    adjoint_y = band_matrix(kernels[1], width_y, width_y, 0, -1)
    adjoint_z = band_matrix(kernels[2], depth_cz, depth_cz + 2 * RADIUS, RADIUS, -1)
    forward_z = band_matrix(kernels[2], depth_cz, depth_cz + 2 * RADIUS, RADIUS, 1)
    estimate = start
    for iteration in range(ITERS):
        widened = with_halo(estimate, (("gz", 0),), RADIUS)
        blurred = apply_depth(apply_planes(widened, forward_x, forward_y), forward_z)
        quotient = recorded.astype(jnp.float32) / blurred
        quotient_wide = with_halo(quotient, (("gz", 0),), RADIUS)
        correction = apply_planes(apply_depth(quotient_wide, adjoint_z), adjoint_x, adjoint_y)
        log_term = jnp.log(correction)
        log_sum = lax.psum(log_term, "view")
        estimate = estimate * jnp.exp(log_sum / view_count)
    return estimate


def solution(mesh):
    in_specs = (P("view", "gz", None, None), P("view", None, None), P("gz", None, None))
    out_specs = P("gz", None, None)
    return jax.shard_map(
        per_device, mesh=mesh, in_specs=in_specs, out_specs=out_specs, check_vma=False
    )
```

profile of v0, /device:TPU:8, one launch (start us, length us, event | category | flops | bytes accessed | tf_op | source)
XLA Modules:
  0.0 712.0 jit_solution(17776579453479125774)
XLA Ops:
  12.2 7.5 %collective-permute-start.1 = (f32[15,128,256]{2,1,0:T(8,128)S(1)}, f32[15,128,256]{2,1,0:T(8,128)}, u32[]{:S(2)}, u32[]{:S(2)}) collective-permute-start(f32[15,128,256]{2,1,0:T(8,128)S(1)} %get-tuple-element.18), channel_id=1, source_target_pairs={{1,0},{2,1},{3,2},{4,3},{5,4},{6,5},{7,6},{8,7},{9,8},{10,9},{11,1... | collective-permute-start | bytes 5898248 | tf_op jit(solution)/shard_map/ppermute | solution.py:19
  22.4 28.7 %collective-permute-done = f32[15,128,256]{2,1,0:T(8,128)} collective-permute-done((f32[15,128,256]{2,1,0:T(8,128)}, f32[15,128,256]{2,1,0:T(8,128)}, u32[]{:S(2)}, u32[]{:S(2)}) %collective-permute-start) | collective-permute-done | bytes 1966112 | tf_op jit(solution)/shard_map/ppermute | solution.py:16
  51.1 11.9 %collective-permute-done.1 = f32[15,128,256]{2,1,0:T(8,128)} collective-permute-done((f32[15,128,256]{2,1,0:T(8,128)S(1)}, f32[15,128,256]{2,1,0:T(8,128)}, u32[]{:S(2)}, u32[]{:S(2)}) %collective-permute-start.1) | collective-permute-done | bytes 1966112 | tf_op jit(solution)/shard_map/ppermute | solution.py:19
  63.0 9.8 %fusion.16 = f32[128,62,256]{2,0,1:T(8,128)S(1)} fusion(f32[15,128,256]{2,1,0:T(8,128)} %collective-permute-done.1, f32[32,128,256]{2,1,0:T(8,128)} %param.5, f32[15,128,256]{2,1,0:T(8,128)} %collective-permute-done, f32[128,128]{1,0:T(8,128)S(1)} %get-tuple-element.8), kind=kOutput, calls=%fused_computation.16 | convolution fusion | flops 3124625408 | bytes 16318464 | tf_op jit(solution)/shard_map/zxy,ox->zoy/dot_general | solution.py:35
  72.9 6.5 fusion.30
  79.4 11.2 %convert_divide_fusion.1 = f32[32,128,256]{2,0,1:T(8,128)S(1)} fusion(f32[62,128,256]{2,1,0:T(8,128)S(1)} %fusion.30, bf16[1,32,128,256]{3,2,1,0:T(8,128)(2,1)S(1)} %copy-done.2, f32[32,62]{1,0:T(8,128)S(1)} %get-tuple-element.10), kind=kOutput, calls=%fused_computation.37 | convolution fusion | flops 782237696 | bytes 14425856 | tf_op jit(solution)/shard_map/zxy,oz->oxy/dot_general | solution.py:40
  92.3 7.0 collective-permute-start.3
  102.5 34.0 %collective-permute-done.3 = f32[15,128,256]{2,1,0:T(8,128)S(1)} collective-permute-done((f32[15,128,256]{2,1,0:T(8,128)S(1)}, f32[15,128,256]{2,1,0:T(8,128)S(1)}, u32[]{:S(2)}, u32[]{:S(2)}) %collective-permute-start.3) | collective-permute-done | bytes 1966112 | tf_op jit(solution)/shard_map/ppermute | solution.py:19
  137.7 7.5 %collective-permute-done.2 = f32[15,128,256]{2,1,0:T(8,128)S(1)} collective-permute-done((f32[15,128,256]{2,1,0:T(8,128)S(1)}, f32[15,128,256]{2,1,0:T(8,128)S(1)}, u32[]{:S(2)}, u32[]{:S(2)}) %collective-permute-start.2) | collective-permute-done | bytes 1966112 | tf_op jit(solution)/shard_map/ppermute | solution.py:16
  146.3 5.5 fusion
  151.8 6.5 fusion.38
  163.4 191.7 %all-reduce.3.cloned.1.call-done = f32[32,128,256]{2,1,0:T(8,128)} async-done(((f32[32,128,256]{2,1,0:T(8,128)}), f32[32,128,256]{2,1,0:T(8,128)}) %all-reduce.3.cloned.1.call-update) | async-done | bytes 4194320 | tf_op jit(solution)/shard_map/psum | solution.py:62
  361.7 6.7 collective-permute-start.5
  368.3 26.8 %collective-permute-done.4 = f32[15,128,256]{2,1,0:T(8,128)S(1)} collective-permute-done((f32[15,128,256]{2,1,0:T(8,128)S(1)}, f32[15,128,256]{2,1,0:T(8,128)S(1)}, u32[]{:S(2)}, u32[]{:S(2)}) %collective-permute-start.4) | collective-permute-done | bytes 1966112 | tf_op jit(solution)/shard_map/ppermute | solution.py:16
  395.1 16.3 %collective-permute-done.5 = f32[15,128,256]{2,1,0:T(8,128)S(1)} collective-permute-done((f32[15,128,256]{2,1,0:T(8,128)S(1)}, f32[15,128,256]{2,1,0:T(8,128)S(1)}, u32[]{:S(2)}, u32[]{:S(2)}) %collective-permute-start.5) | collective-permute-done | bytes 1966112 | tf_op jit(solution)/shard_map/ppermute | solution.py:19
  411.4 7.3 %fusion.22 = f32[128,62,256]{2,0,1:T(8,128)S(1)} fusion(f32[15,128,256]{2,1,0:T(8,128)S(1)} %collective-permute-done.5, f32[32,128,256]{2,1,0:T(8,128)S(1)} %exponential_multiply_fusion.1, f32[15,128,256]{2,1,0:T(8,128)S(1)} %collective-permute-done.4, f32[128,128]{1,0:T(8,128)S(1)} %get-tuple-element.8), kind=kOutput, calls=%fused_computation.22 | convolution fusion | flops 3124625408 | bytes 16318464 | tf_op jit(solution)/shard_map/zxy,ox->zoy/dot_general | solution.py:35
  418.8 6.7 fusion.28
  425.5 11.0 %convert_divide_fusion = f32[32,128,256]{2,0,1:T(8,128)S(1)} fusion(f32[62,128,256]{2,1,0:T(8,128)S(1)} %fusion.28, bf16[1,32,128,256]{3,2,1,0:T(8,128)(2,1)S(1)} %copy-done.3, f32[32,62]{1,0:T(8,128)S(1)} %get-tuple-element.10), kind=kOutput, calls=%fused_computation.36 | convolution fusion | flops 782237696 | bytes 14425856 | tf_op jit(solution)/shard_map/zxy,oz->oxy/dot_general | solution.py:40
  438.1 6.8 collective-permute-start.7
  448.0 33.5 %collective-permute-done.7 = f32[15,128,256]{2,1,0:T(8,128)S(1)} collective-permute-done((f32[15,128,256]{2,1,0:T(8,128)S(1)}, f32[15,128,256]{2,1,0:T(8,128)S(1)}, u32[]{:S(2)}, u32[]{:S(2)}) %collective-permute-start.7) | collective-permute-done | bytes 1966112 | tf_op jit(solution)/shard_map/ppermute | solution.py:19
  482.7 10.4 %collective-permute-done.6 = f32[15,128,256]{2,1,0:T(8,128)S(1)} collective-permute-done((f32[15,128,256]{2,1,0:T(8,128)S(1)}, f32[15,128,256]{2,1,0:T(8,128)S(1)}, u32[]{:S(2)}, u32[]{:S(2)}) %collective-permute-start.6) | collective-permute-done | bytes 1966112 | tf_op jit(solution)/shard_map/ppermute | solution.py:16
  499.8 6.4 fusion.36
  511.2 187.2 %all-reduce.5.cloned.1.call-done = f32[32,128,256]{2,1,0:T(8,128)} async-done(((f32[32,128,256]{2,1,0:T(8,128)}), f32[32,128,256]{2,1,0:T(8,128)}) %all-reduce.5.cloned.1.call-update) | async-done | bytes 4194320 | tf_op jit(solution)/shard_map/psum | solution.py:62
  698.4 6.4 exponential_multiply_fusion
  (41 shorter events, 44.5 us)
Async XLA Ops:
  6.5 13.3 %copy-start.1 = (f32[1,3,31]{2,0,1:T(1,128)S(1)}, f32[1,3,31]{2,0,1:T(1,128)}, u32[]{:S(2)}) copy-start(f32[1,3,31]{2,0,1:T(1,128)} %param.4) | copy-start | bytes 1120
  6.5 348.6 %all-reduce.3.cloned.1.call-start = ((), (), s32[]{:S(2)}) async-start(), calls=%async_computation | async-start | bytes 8388608 | tf_op jit(solution)/shard_map/psum | solution.py:62
  10.3 40.8 %collective-permute-start = (f32[15,128,256]{2,1,0:T(8,128)}, f32[15,128,256]{2,1,0:T(8,128)}, u32[]{:S(2)}, u32[]{:S(2)}) collective-permute-start(f32[15,128,256]{2,1,0:T(8,128)} %get-tuple-element.17), channel_id=1, source_target_pairs={{0,1},{1,2},{2,3},{3,4},{4,5},{5,6},{6,7},{7,8},{8,9},{9,10},{10,1... | collective-permute-start | bytes 5898248 | tf_op jit(solution)/shard_map/ppermute | solution.py:16
  12.2 50.8 %collective-permute-start.1 = (f32[15,128,256]{2,1,0:T(8,128)S(1)}, f32[15,128,256]{2,1,0:T(8,128)}, u32[]{:S(2)}, u32[]{:S(2)}) collective-permute-start(f32[15,128,256]{2,1,0:T(8,128)S(1)} %get-tuple-element.18), channel_id=1, source_target_pairs={{1,0},{2,1},{3,2},{4,3},{5,4},{6,5},{7,6},{8,7},{9,8},{10,9},{11,1... | collective-permute-start | bytes 5898248 | tf_op jit(solution)/shard_map/ppermute | solution.py:19
  72.9 6.5 copy-start.2
  92.3 44.3 %collective-permute-start.3 = (f32[15,128,256]{2,1,0:T(8,128)S(1)}, f32[15,128,256]{2,1,0:T(8,128)S(1)}, u32[]{:S(2)}, u32[]{:S(2)}) collective-permute-start(f32[15,128,256]{2,1,0:T(8,128)S(1)} %copy.17), channel_id=1, source_target_pairs={{1,0},{2,1},{3,2},{4,3},{5,4},{6,5},{7,6},{8,7},{9,8},{10,9},{11,1... | collective-permute-start | bytes 5898248 | tf_op jit(solution)/shard_map/ppermute | solution.py:19
  100.4 44.8 %collective-permute-start.2 = (f32[15,128,256]{2,1,0:T(8,128)S(1)}, f32[15,128,256]{2,1,0:T(8,128)S(1)}, u32[]{:S(2)}, u32[]{:S(2)}) collective-permute-start(f32[15,128,256]{2,1,0:T(8,128)S(1)} %copy.16), channel_id=1, source_target_pairs={{0,1},{1,2},{2,3},{3,4},{4,5},{5,6},{6,7},{7,8},{8,9},{9,10},{10,1... | collective-permute-start | bytes 5898248 | tf_op jit(solution)/shard_map/ppermute | solution.py:16
  163.4 535.0 %all-reduce.5.cloned.1.call-start = ((), (), s32[]{:S(2)}) async-start(), calls=%async_computation.1 | async-start | bytes 8388608 | tf_op jit(solution)/shard_map/psum | solution.py:62
  359.5 59.3 %copy-start = (f32[32,128,256]{2,1,0:T(8,128)}, f32[32,128,256]{2,1,0:T(8,128)S(1)}, u32[]{:S(2)}) copy-start(f32[32,128,256]{2,1,0:T(8,128)S(1)} %exponential_multiply_fusion.1) | copy-start | bytes 12582916
  359.8 35.4 %collective-permute-start.4 = (f32[15,128,256]{2,1,0:T(8,128)S(1)}, f32[15,128,256]{2,1,0:T(8,128)S(1)}, u32[]{:S(2)}, u32[]{:S(2)}) collective-permute-start(f32[15,128,256]{2,1,0:T(8,128)S(1)} %get-tuple-element.13), channel_id=1, source_target_pairs={{0,1},{1,2},{2,3},{3,4},{4,5},{5,6},{6,7},{7,8},{8,9},{9,10},{10,1... | collective-permute-start | bytes 5898248 | tf_op jit(solution)/shard_map/ppermute | solution.py:16
  361.7 49.7 %collective-permute-start.5 = (f32[15,128,256]{2,1,0:T(8,128)S(1)}, f32[15,128,256]{2,1,0:T(8,128)S(1)}, u32[]{:S(2)}, u32[]{:S(2)}) collective-permute-start(f32[15,128,256]{2,1,0:T(8,128)S(1)} %get-tuple-element.14), channel_id=1, source_target_pairs={{1,0},{2,1},{3,2},{4,3},{5,4},{6,5},{7,6},{8,7},{9,8},{10,9},{11,1... | collective-permute-start | bytes 5898248 | tf_op jit(solution)/shard_map/ppermute | solution.py:19
  418.7 6.7 copy-start.3
  438.1 43.4 %collective-permute-start.7 = (f32[15,128,256]{2,1,0:T(8,128)S(1)}, f32[15,128,256]{2,1,0:T(8,128)S(1)}, u32[]{:S(2)}, u32[]{:S(2)}) collective-permute-start(f32[15,128,256]{2,1,0:T(8,128)S(1)} %copy.23), channel_id=1, source_target_pairs={{1,0},{2,1},{3,2},{4,3},{5,4},{6,5},{7,6},{8,7},{9,8},{10,9},{11,1... | collective-permute-start | bytes 5898248 | tf_op jit(solution)/shard_map/ppermute | solution.py:19
  446.1 47.0 %collective-permute-start.6 = (f32[15,128,256]{2,1,0:T(8,128)S(1)}, f32[15,128,256]{2,1,0:T(8,128)S(1)}, u32[]{:S(2)}, u32[]{:S(2)}) collective-permute-start(f32[15,128,256]{2,1,0:T(8,128)S(1)} %copy.22), channel_id=1, source_target_pairs={{0,1},{1,2},{2,3},{3,4},{4,5},{5,6},{6,7},{7,8},{8,9},{9,10},{10,1... | collective-permute-start | bytes 5898248 | tf_op jit(solution)/shard_map/ppermute | solution.py:16
Sparse Core Ops, SparseCore 0:
  163.5 191.5 all-reduce.2
  511.3 186.9 all-reduce.4
where the time goes:
time: 718 us; the launch traced here: 712 us
  waiting for transfers between devices  548 us (76%)
  matrix products  86.5 us (12%)
  starting transfers between devices  35.9 us (5%)
  local copies, waits for them, and re-layouts  14.1 us (2%)
  between operations  14.1 us (2%)
  other arithmetic  13.3 us (2%)
    psum x2, waiting for transfers between devices, per_device(): log_sum = lax.psum(log_term, 'view')  379 us
    ppermute x4, waiting for transfers between devices, with_halo(): lax.ppermute(lax.slice_in_dim(block, 0, width, axis=dim), axis, backward)  95.8 us
    ppermute x4, waiting for transfers between devices, with_halo(): lax.ppermute(lax.slice_in_dim(block, block.shape[dim] - width, None, axis...  73.4 us
    dot_general x4, matrix products, apply_depth(): jnp.einsum('zxy,oz->oxy', volume, matrix_z, precision=lax.Precision.HIGHEST)  33.2 us
    dot_general x4, matrix products, apply_planes(): jnp.einsum('zxy,ox->zoy', volume, matrix_x, precision=lax.Precision.HIGHEST)  30 us
    ppermute x4, starting transfers between devices, with_halo(): lax.ppermute(lax.slice_in_dim(block, 0, width, axis=dim), axis, backward)  28 us
    dot_general x4, matrix products, apply_planes(): jnp.einsum('zxy,oy->zxo', volume, matrix_y, precision=lax.Precision.HIGHEST)  23.3 us
  transfers between devices with their start and end apart: 10, of which 10 were waited for; matrix products, arithmetic and copies ran while one was open for 1% of the time, Pallas kernels for 0%

commit v1 on v0

v1 whole, which is shorter than its diff:
```python
import jax
import jax.numpy as jnp
import numpy as np
from jax import lax
from jax.experimental import pallas as pl
from jax.experimental.pallas import tpu as pltpu
from jax.sharding import PartitionSpec as P

RADIUS = 15
TAPS = 31
ITERS = 2
F32, BF16 = jnp.float32, jnp.bfloat16
GROUP = 8

_PHASE = np.arange(16)[:, None] * 0.7548776662 + np.arange(256)[None, :] * 0.5698402909
SPREAD = (1.0 + _PHASE % 1.0).astype(np.float32)
UNSPREAD = (1.0 / SPREAD.astype(np.float64)).astype(np.float32)


def call(kernel, outs, args, scratch=(), smem=0):
    specs = [pl.BlockSpec(memory_space=pltpu.SMEM)] * smem
    specs += [pl.BlockSpec(memory_space=pltpu.VMEM)] * (len(args) - smem)
    return pl.pallas_call(
        kernel,
        out_shape=[jax.ShapeDtypeStruct(shape, dtype) for shape, dtype in outs],
        in_specs=specs,
        out_specs=[pl.BlockSpec(memory_space=pltpu.VMEM)] * len(outs),
        scratch_shapes=list(scratch),
        compiler_params=pltpu.CompilerParams(vmem_limit_bytes=40 * 1024 * 1024),
        cost_estimate=pl.CostEstimate(flops=1000, bytes_accessed=1000, transcendentals=0),
    )(*args)


def split(a):
    high = a.astype(BF16)
    return high, (a - high.astype(F32)).astype(BF16)


def mul(a, b):
    return jnp.dot(a, b, preferred_element_type=F32)


def mul3(a, b):
    return mul(a[0], b[0]) + mul(a[0], b[1]) + mul(a[1], b[0])


def tile_rows(pattern, rows):
    return jnp.concatenate([pattern] * (rows // pattern.shape[0]), axis=0)


def band_kernel(n_near, n_far, core_ref, taps_ref, *outs):
    depth = n_near + n_far
    core = core_ref[0]
    near_at, far_at = (depth - n_near) * core, (depth - n_far) * (1 - core)
    natural = lambda i: i
    ordered = lambda i: jnp.where(i < n_far, far_at + i, near_at + i - n_far)
    near = lambda i: near_at + i
    ext = lambda i: i + jnp.where(core == 0, -n_near, depth)
    sib = lambda i: i + jnp.where(core == 0, depth, -n_far)
    plans = [
        (0, natural, natural, 1, 1), (0, natural, natural, -1, 1),
        (1, natural, natural, -1, 1), (1, natural, natural, 1, 1),
        (2, ordered, natural, 1, GROUP), (2, ordered, sib, 1, GROUP), (2, near, ext, 1, GROUP),
        (2, ordered, ordered, -1, GROUP), (2, ordered, sib, -1, GROUP), (2, near, ext, -1, GROUP),
    ]
    for out, (axis, out_pos, in_pos, direction, repeat) in zip(outs, plans):
        row = lax.broadcasted_iota(jnp.int32, out.shape, 0)
        column = lax.broadcasted_iota(jnp.int32, out.shape, 1)
        tap = direction * (in_pos(column // repeat) - out_pos(row // repeat)) + RADIUS
        if repeat > 1:
            tap = jnp.where(row % repeat == column % repeat, tap, -1)
        total = jnp.zeros(out.shape, F32)
        for k in range(TAPS):
            total = total + jnp.where(tap == k, taps_ref[axis, k], 0.0)
        out[...] = total


def blur_rows(planes, mx, my):
    return mul3(split(mul3(mx, split(planes))), my)


def z_rows(own, sib_ref, at, half, wo, ws, unspread):
    n_sib = sib_ref.shape[0]
    total = mul3(wo, split(own))
    sib = sib_ref[:, pl.ds(at, 16), :].astype(F32)[:, half * GROUP:(half + 1) * GROUP]
    sib = jnp.concatenate(
        [sib.reshape(n_sib * GROUP, -1), jnp.zeros((ws[0].shape[1] - n_sib * GROUP, sib.shape[2]), F32)], axis=0
    ).astype(BF16)
    other = mul(ws[0], sib) + mul(ws[1], sib)
    scale = unspread[half * GROUP:(half + 1) * GROUP]
    return total + other * tile_rows(scale, other.shape[0])


def fill_z(own_refs, sib_ref, wo_ref, ws_ref, unspread_ref, far_ref, near_ref):
    wo, ws, unspread = split(wo_ref[...]), split(ws_ref[...]), unspread_ref[...]
    nx, ny = far_ref.shape[1:]

    def step(g, _):
        at = pl.multiple_of(g * 16, 16)
        for half in range(2):
            here = pl.ds(pl.multiple_of(at + half * GROUP, GROUP), GROUP)
            own = jnp.concatenate([r[:, here, :].reshape(r.shape[0] * GROUP, ny) for r in own_refs], axis=0)
            out = z_rows(own, sib_ref, at, half, wo, ws, unspread)
            cut = far_ref.shape[0] * GROUP
            far_ref[:, here, :] = out[:cut].reshape(far_ref.shape[0], GROUP, ny)
            near_ref[:, here, :] = out[cut:].reshape(near_ref.shape[0], GROUP, ny)
        return 0

    lax.fori_loop(0, nx // 16, step, 0)


def add_ext(ext_ref, we_ref, unspread_ref, near_ref, out_ref):
    we, unspread = split(we_ref[...]), unspread_ref[...]
    n, nx, ny = near_ref.shape

    def step(g, _):
        at = pl.multiple_of(g * 16, 16)
        block = ext_ref[:, pl.ds(at, 16), :].astype(F32)
        for half in range(2):
            here = pl.ds(pl.multiple_of(at + half * GROUP, GROUP), GROUP)
            ext = block[:, half * GROUP:(half + 1) * GROUP].reshape(n * GROUP, ny)
            ext = jnp.concatenate([ext, jnp.zeros((we[0].shape[1] - n * GROUP, ny), F32)], axis=0).astype(BF16)
            other = (mul(we[0], ext) + mul(we[1], ext))[:n * GROUP]
            other = other * tile_rows(unspread[half * GROUP:(half + 1) * GROUP], n * GROUP)
            out_ref[:, here, :] = near_ref[:, here, :] + other.reshape(n, GROUP, ny)
        return 0

    lax.fori_loop(0, nx // 16, step, 0)


def to_quotient(load, count, recorded_ref, mx_ref, my_ref, spread_ref, quotient_ref, wire_ref):
    mx, my = split(mx_ref[...]), split(my_ref[...])
    pattern = tile_rows(spread_ref[...], recorded_ref.shape[1])

    def step(p, _):
        quotient = recorded_ref[p].astype(F32) / blur_rows(load(p), mx, my)
        quotient_ref[p] = quotient
        wire_ref[p] = (quotient * pattern).astype(BF16)
        return 0

    lax.fori_loop(0, count, step, 0)


def to_log(load, count, mx_ref, my_ref, log_ref):
    mx, my = split(mx_ref[...]), split(my_ref[...])
    views, _, rows, ny = log_ref.shape

    def step(p, _):
        log_ref[:, p] = jnp.log(blur_rows(load(p), mx, my)).reshape(views, rows, ny)
        return 0

    lax.fori_loop(0, count, step, 0)


def first_far_kernel(start_ref, sib_ref, wo_ref, ws_ref, unspread_ref, recorded_ref, mx_ref, my_ref, spread_ref,
                     quotient_ref, wire_ref, near_ref, far_ref):
    fill_z([start_ref], sib_ref, wo_ref, ws_ref, unspread_ref, far_ref, near_ref)
    to_quotient(lambda p: far_ref[p], quotient_ref.shape[0], recorded_ref, mx_ref, my_ref, spread_ref, quotient_ref, wire_ref)


def first_near_kernel(near_ref, ext_ref, we_ref, unspread_ref, recorded_ref, mx_ref, my_ref, spread_ref,
                      quotient_ref, wire_ref, sum_ref):
    add_ext(ext_ref, we_ref, unspread_ref, near_ref, sum_ref)
    to_quotient(lambda p: sum_ref[p], quotient_ref.shape[0], recorded_ref, mx_ref, my_ref, spread_ref, quotient_ref, wire_ref)


def block_kernel(first, blocks_ref, unspread_ref, recorded_ref, mx_ref, my_ref, spread_ref, quotient_ref, wire_ref):
    views, _, rows, ny = blocks_ref.shape
    pattern = tile_rows(unspread_ref[...], views * rows)

    def load(p):
        return blocks_ref[:, first + p].reshape(views * rows, ny).astype(F32) * pattern

    to_quotient(load, quotient_ref.shape[0], recorded_ref, mx_ref, my_ref, spread_ref, quotient_ref, wire_ref)


def adjoint_far_kernel(far_q_ref, near_q_ref, sib_ref, wo_ref, ws_ref, unspread_ref, mx_ref, my_ref, log_ref, near_ref, far_ref):
    fill_z([far_q_ref, near_q_ref], sib_ref, wo_ref, ws_ref, unspread_ref, far_ref, near_ref)
    to_log(lambda p: far_ref[p], far_ref.shape[0], mx_ref, my_ref, log_ref)


def adjoint_near_kernel(near_ref, ext_ref, _, we_ref, unspread_ref, mx_ref, my_ref, log_ref, sum_ref):
    add_ext(ext_ref, we_ref, unspread_ref, near_ref, sum_ref)
    to_log(lambda p: sum_ref[p], sum_ref.shape[0], mx_ref, my_ref, log_ref)


def assemble_kernel(blocks_ref, out_ref):
    depth, rows, ny = out_ref.shape
    for z in range(depth):
        exponent = blocks_ref[0, depth + z // rows, z % rows:z % rows + 1, :]
        out_ref[z] = blocks_ref[0, z] * jnp.exp2(exponent - 15.0)


def assemble(blocks, depth):
    views, planes, rows, ny = blocks.shape
    return pl.pallas_call(
        assemble_kernel,
        grid=(views,),
        out_shape=jax.ShapeDtypeStruct((depth, views * rows, ny), F32),
        in_specs=[pl.BlockSpec((1, planes, rows, ny), lambda j: (j, 0, 0, 0))],
        out_specs=pl.BlockSpec((depth, rows, ny), lambda j: (0, j, 0)),
        compiler_params=pltpu.CompilerParams(vmem_limit_bytes=20 * 1024 * 1024),
        cost_estimate=pl.CostEstimate(flops=1000, bytes_accessed=1000, transcendentals=0),
    )(blocks)


def to_other_chip(planes):
    count = lax.axis_size("gz")
    pairs = [(i, i + 1) for i in range(1, count - 1, 2)]
    return lax.ppermute(planes, "gz", pairs + [(b, a) for a, b in pairs])


def to_sibling(planes):
    count = lax.axis_size("gz")
    return lax.ppermute(planes, "gz", [(i, i ^ 1) for i in range(count)])


def to_views(blocks):
    return lax.all_to_all(blocks, "view", 0, 0)


def sum_over_views(log_blocks):
    return jnp.sum(to_views(log_blocks.astype(jnp.float16)).astype(F32), axis=0)


def band(kernel_row, out_pos, in_pos):
    tap_index = in_pos[None, :] - out_pos[:, None] + RADIUS
    one_hot = (tap_index[:, :, None] == jnp.arange(TAPS, dtype=jnp.int32)[None, None, :]).astype(F32)
    return jnp.sum(one_hot * kernel_row[None, None, :], axis=2)


def gather_result(piece):
    views = lax.axis_size("view")
    depth, rows, ny = piece.shape
    extra = -(-depth // rows)
    exponent = jnp.maximum(jnp.ceil(jnp.log2(jnp.max(piece, axis=(1, 2)))), -100.0)
    scaled = piece * jnp.exp2(15.0 - exponent)[:, None, None]
    note = jnp.pad(exponent, (0, extra * rows - depth)).reshape(extra, rows, 1)
    note = jnp.broadcast_to(note, (extra, rows, ny))
    wire = jnp.concatenate([scaled, note], axis=0).astype(jnp.float16)
    return assemble(to_views(jnp.broadcast_to(wire[None], (views,) + wire.shape)).astype(F32), depth)


def per_device(views_data, psf, start):
    kernels = psf[0] / jnp.sum(psf[0], axis=1, keepdims=True)
    recorded = views_data[0]
    depth, nx, ny = recorded.shape
    views = lax.axis_size("view")
    v = lax.axis_index("view")
    core = lax.axis_index("gz") % 2
    rows = nx // views
    n_near, n_far = RADIUS, depth - RADIUS
    spread, unspread = jnp.asarray(SPREAD), jnp.asarray(UNSPREAD)

    near_at, far_at = (depth - n_near) * core, (depth - n_far) * (1 - core)

    def near_of(a):
        return lax.dynamic_slice_in_dim(a, near_at, n_near, axis=0)

    def far_of(a):
        return lax.dynamic_slice_in_dim(a, far_at, n_far, axis=0)

    def to_wire(planes):
        count = planes.shape[-2] // spread.shape[0]
        return (planes * jnp.concatenate([spread] * count, axis=0)).astype(BF16)

    ext = to_other_chip(to_wire(near_of(start)))
    sib = to_sibling(to_wire(far_of(start)))

    full, wide, small = depth * GROUP, 256, 128
    near_rows = n_near * GROUP
    matrices = call(
        lambda *refs: band_kernel(n_near, n_far, *refs),
        [((nx, nx), F32)] * 2 + [((ny, ny), F32)] * 2
        + [((full, full), F32), ((full, 144), F32), ((near_rows, small), F32)] * 2,
        [core.reshape(1).astype(jnp.int32), kernels],
        smem=2,
    )
    forward_x, adjoint_x, forward_y, adjoint_y, forward_o, forward_s, forward_e, adjoint_o, adjoint_s, adjoint_e = matrices

    own_rows = lax.dynamic_slice_in_dim(start, v * rows, rows, axis=1)
    piece_far, piece_near = far_of(own_rows), near_of(own_rows)
    recorded_far, recorded_near = far_of(recorded), near_of(recorded)

    count = jnp.arange(depth, dtype=jnp.int32)
    out_z = jnp.where(count < n_far, far_at + count, near_at + count - n_far)
    sib_z = count[:n_far] + jnp.where(core == 0, depth, -n_far)
    ext_z = count[:n_near] + jnp.where(core == 0, -n_near, depth)
    wide_z = jnp.concatenate([out_z, sib_z, ext_z])
    every_z = jnp.broadcast_to(jnp.pad(kernels[2], (0, 128 - TAPS)), (views, GROUP, 128))
    every_z = to_views(every_z)[:, 0, :TAPS]
    forward_all = jax.vmap(lambda kernel_row: band(kernel_row, out_z, wide_z))(every_z)

    far_shape, near_shape = (n_far, nx, ny), (n_near, nx, ny)
    quotient_far, wire_far, partly = call(
        first_far_kernel,
        [(far_shape, F32), (far_shape, BF16), (near_shape, F32)],
        [start, sib, forward_o, forward_s, unspread, recorded_far, forward_x, forward_y, spread],
        [pltpu.VMEM(far_shape, F32)],
    )
    sib = to_sibling(wire_far)
    quotient_near, wire_near = call(
        first_near_kernel,
        [(near_shape, F32), (near_shape, BF16)],
        [partly, ext, forward_e, unspread, recorded_near, forward_x, forward_y, spread],
        [pltpu.VMEM(near_shape, F32)],
    )
    ext = to_other_chip(wire_near)

    for iteration in range(ITERS):
        log_far, partly = call(
            adjoint_far_kernel,
            [((views, n_far, rows, ny), F32), (near_shape, F32)],
            [quotient_far, quotient_near, sib, adjoint_o, adjoint_s, unspread, adjoint_x, adjoint_y],
            [pltpu.VMEM(far_shape, F32)],
        )
        sum_far = sum_over_views(log_far)
        piece_far = piece_far * jnp.exp(sum_far / views)

        (log_near,) = call(
            adjoint_near_kernel,
            [((views, n_near, rows, ny), F32)],
            [partly, ext, sum_far[0, :8], adjoint_e, unspread, adjoint_x, adjoint_y],
            [pltpu.VMEM(near_shape, F32)],
        )
        piece_near = piece_near * jnp.exp(sum_over_views(log_near) / views)

        if iteration < ITERS - 1:
            ext = to_other_chip(to_wire(piece_near))
            sib = to_sibling(to_wire(piece_far))
            planes = jnp.concatenate(
                [piece_far, piece_near, sib.astype(F32) * unspread, ext.astype(F32) * unspread], axis=0
            )
            blocks = jnp.einsum("zxy,voz->voxy", planes, forward_all, precision=lax.Precision.HIGH)
            blocks = to_views(to_wire(blocks))
            quotient_near, wire_near = call(
                lambda *refs: block_kernel(n_far, *refs),
                [(near_shape, F32), (near_shape, BF16)],
                [blocks, unspread, recorded_near, forward_x, forward_y, spread],
            )
            ext = to_other_chip(wire_near)
            quotient_far, wire_far = call(
                lambda *refs: block_kernel(0, *refs),
                [(far_shape, F32), (far_shape, BF16)],
                [blocks, unspread, recorded_far, forward_x, forward_y, spread],
            )
            sib = to_sibling(wire_far)

    both = jnp.concatenate([piece_near, piece_far, piece_near], axis=0)
    return gather_result(lax.dynamic_slice_in_dim(both, n_near * core, depth, axis=0))


def solution(mesh):
    in_specs = (P("view", "gz", None, None), P("view", None, None), P("gz", None, None))
    out_specs = P("gz", None, None)
    return jax.shard_map(
        per_device, mesh=mesh, in_specs=in_specs, out_specs=out_specs, check_vma=False
    )
```

time: 718 us -> 339 us (0.47)
  waiting for transfers between devices: 548 us -> 109 us
  Pallas kernels: 0 us -> 85.7 us
  matrix products: 86.5 us -> 2.06 us
  blocking collectives: 0 us -> 58.3 us
  between operations: 14.1 us -> 0.62 us
  starting transfers between devices: 35.9 us -> 46.6 us
    psum x2 -> x0, waiting for transfers between devices: 379 us -> none  [per_device(): log_sum = lax.psum(log_term, 'view')]
    ppermute x8, waiting for transfers between devices: 169 us -> 41.9 us  [the longest x4 41.8 us: to_other_chip(): return lax.ppermute(planes, 'gz', pairs + [(b, a) for a, b in pairs])]
    pallas_call x0 -> x10, Pallas kernels: none -> 85.7 us  [the longest x9 82.2 us: call(): pl.pallas_call(kernel, out_shape=[jax.ShapeDtypeStruct(shape, dtype) for...]
    dot_general x12 -> x1, matrix products: 86.5 us -> 2.06 us  [per_device(): jnp.einsum('zxy,voz->voxy', planes, forward_all, precision=lax.Precision....]
    all_to_all x0 -> x5, waiting for transfers between devices: none -> 67.4 us  [to_views(): return lax.all_to_all(blocks, 'view', 0, 0)]
    all_to_all x0 -> x2, blocking collectives: none -> 58.3 us  [to_views(): return lax.all_to_all(blocks, 'view', 0, 0)]
    all_to_all x0 -> x5, starting transfers between devices: none -> 25 us  [to_views(): return lax.all_to_all(blocks, 'view', 0, 0)]
    ppermute x8, starting transfers between devices: 35.8 us -> 21.6 us  [the longest x4 20.9 us: to_other_chip(): return lax.ppermute(planes, 'gz', pairs + [(b, a) for a, b in pairs])]
  transfers between devices with their start and end apart: 10 -> 13, of which waited for: 10 -> 8; matrix products, arithmetic and copies ran while one was open for 1% -> 3% of each run, Pallas kernels for 0% -> 9%
where the time goes in v1:
time: 339 us; the launch traced here: 338 us
  waiting for transfers between devices  109 us (32%)
  Pallas kernels  85.7 us (25%)
  blocking collectives  58.3 us (17%)
  starting transfers between devices  46.6 us (14%)
  other arithmetic  19.6 us (6%)
  local copies, waits for them, and re-layouts  15.3 us (5%)
    pallas_call x9, Pallas kernels, call(): pl.pallas_call(kernel, out_shape=[jax.ShapeDtypeStruct(shape, dtype) for...  82.2 us
    all_to_all x5, waiting for transfers between devices, to_views(): return lax.all_to_all(blocks, 'view', 0, 0)  67.4 us
    all_to_all x2, blocking collectives, to_views(): return lax.all_to_all(blocks, 'view', 0, 0)  58.3 us
    ppermute x4, waiting for transfers between devices, to_other_chip(): return lax.ppermute(planes, 'gz', pairs + [(b, a) for a, b in pairs])  41.8 us
    all_to_all x5, starting transfers between devices, to_views(): return lax.all_to_all(blocks, 'view', 0, 0)  25 us
    ppermute x4, starting transfers between devices, to_other_chip(): return lax.ppermute(planes, 'gz', pairs + [(b, a) for a, b in pairs])  20.9 us
    unnamed x90, local copies, waits for them, and re-layouts  13.5 us
    convert_element_type x5, other arithmetic, to_wire(): return (planes * jnp.concatenate([spread] * count, axis=0)).astype(BF16)  8.33 us
  transfers between devices with their start and end apart: 13, of which 8 were waited for; matrix products, arithmetic and copies ran while one was open for 3% of the time, Pallas kernels for 9%

profile of v1, /device:TPU:8, one launch (start us, length us, event | category | flops | bytes accessed | tf_op | source)
XLA Modules:
  0.0 337.5 jit_solution(13028812635110784294)
XLA Ops:
  3.2 5.7 %shard_map.55 = (f32[128,128]{1,0:T(8,128)S(1)}, f32[128,128]{1,0:T(8,128)S(1)}, f32[256,256]{1,0:T(8,128)S(1)}, f32[256,256]{1,0:T(8,128)S(1)}, f32[256,256]{1,...) custom-call(s32[1]{0:T(128)} %bitcast.refs_0_, ...), custom_call_target="tpu_custom_call" | custom-call | flops 1000 | bytes 1000 | tf_op jit(solution)/shard_map/pallas_call | solution.py:23
  19.0 12.8 %shard_map.56 = (f32[17,128,256]{2,1,0:T(8,128)S(1)}, bf16[17,128,256]{2,1,0:T(8,128)(2,1)S(1)}, f32[15,128,256]{2,1,0:T(8,128)S(1)}) custom-call(f32[32,128,256]{2,1,0:T(8,128)S(1)} %copy-done.2, bf16[17,128,256]{2,1,0:T(8,128)(2,1)} %collective-permute-done.sib_ref, f32[256,256]{1,0:T(8,128)S(1)} %copy-done.25, f32[256,144]{1,0:T(8,128)S(1)} %copy-done.27, ...), custom_call_target="tpu_custom_call" | custom-call | flops 1000 | bytes 1000 | tf_op jit(solution)/shard_map/pallas_call | solution.py:23
  32.6 7.7 %collective-permute-start.1 = (bf16[15,128,256]{2,1,0:T(8,128)(2,1)S(1)}, bf16[15,128,256]{2,1,0:T(8,128)(2,1)S(1)}, u32[]{:S(2)}, u32[]{:S(2)}) collective-permute-start(bf16[15,128,256]{2,1,0:T(8,128)(2,1)S(1)} %multiply_convert_fusion.1), channel_id=1, source_target_pairs={{1,2},{3,4},{5,6},{7,8},{9,10},{11,12},{13,14},{15,16},{17,18},{19... | collective-permute-start | bytes 2949128 | tf_op jit(solution)/shard_map/ppermute | solution.py:210
  40.5 22.1 %collective-permute-done.1.ext_ref = bf16[15,128,256]{2,1,0:T(8,128)(2,1)S(1)} collective-permute-done((bf16[15,128,256]{2,1,0:T(8,128)(2,1)S(1)}, bf16[15,128,256]{2,1,0:T(8,128)(2,1)S(1)}, u32[]{:S(2)}, u32[]{:S(2)}) %collective-permute-start.1) | collective-permute-done | bytes 983072 | tf_op jit(solution)/shard_map/ppermute | solution.py:210
  62.6 8.4 %shard_map.57 = (f32[15,128,256]{2,1,0:T(8,128)S(1)}, bf16[15,128,256]{2,1,0:T(8,128)(2,1)S(1)}) custom-call(f32[15,128,256]{2,1,0:T(8,128)S(1)} %get-tuple-element.33.near_ref, bf16[15,128,256]{2,1,0:T(8,128)(2,1)S(1)} %collective-permute-done.1.ext_ref, f32[120,128]{1,0:T(8,128)S(1)} %copy-done.31, f32[16,256]{1,0:T(8,128)S(1)} %copy-done.12, ...), custom_call_target="tpu_custom_call" | custom-call | flops 1000 | bytes 1000 | tf_op jit(solution)/shard_map/pallas_call | solution.py:23
  71.0 11.5 %shard_map.58 = (f32[8,17,16,256]{3,2,1,0:T(8,128)S(1)}, f32[15,128,256]{2,1,0:T(8,128)S(1)}) custom-call(f32[17,128,256]{2,1,0:T(8,128)S(1)} %get-tuple-element.32.far_q_ref, f32[15,128,256]{2,1,0:T(8,128)S(1)} %get-tuple-element.35.near_q_ref, bf16[17,128,256]{2,1,0:T(8,128)(2,1)S(1)} %collective-permute-done.2.sib_ref, f32[256,256]{1,0:T(8,128)S(1)} %copy-done.17, ...), custom_call_target="tpu_custom_call" | custom-call | flops 1000 | bytes 1000 | tf_op jit(solution)/shard_map/pallas_call | solution.py:23
  85.1 5.0 %all-to-all-start = ((f16[8,17,16,256]{3,2,1,0:T(8,128)(2,1)}), f16[8,17,16,256]{3,2,1,0:T(8,128)(2,1)}, u32[]{:S(2)}, u32[]{:S(2)}) async-start(f16[8,17,16,256]{3,2,1,0:T(8,128)(2,1)} %convert_element_type.64), calls=%async_computation | async-start | bytes 2228224 | tf_op jit(solution)/shard_map/all_to_all | solution.py:219
  90.1 6.2 %collective-permute-start.3 = (bf16[15,128,256]{2,1,0:T(8,128)(2,1)}, bf16[15,128,256]{2,1,0:T(8,128)(2,1)}, u32[]{:S(2)}, u32[]{:S(2)}) collective-permute-start(bf16[15,128,256]{2,1,0:T(8,128)(2,1)} %copy-done.33), channel_id=1, source_target_pairs={{1,2},{3,4},{5,6},{7,8},{9,10},{11,12},{13,14},{15,16},{17,18},{19... | collective-permute-start | bytes 2949128 | tf_op jit(solution)/shard_map/ppermute | solution.py:210
  97.0 17.7 %all-to-all-done = f16[8,17,16,256]{3,2,1,0:T(8,128)(2,1)} async-done(((f16[8,17,16,256]{3,2,1,0:T(8,128)(2,1)}), f16[8,17,16,256]{3,2,1,0:T(8,128)(2,1)}, u32[]{:S(2)}, u32[]{:S(2)}) %all-to-all-start) | async-done | bytes 1114144 | tf_op jit(solution)/shard_map/all_to_all | solution.py:219
  115.3 6.1 %all-to-all-start.2 = ((f32[8,8,128]{2,1,0:T(8,128)}), f32[8,8,128]{2,1,0:T(8,128)S(1)}, u32[]{:S(2)}, u32[]{:S(2)}) async-start(f32[8,8,128]{2,1,0:T(8,128)} %broadcast_in_dim.6), calls=%async_computation.2 | async-start | bytes 65536 | tf_op jit(solution)/shard_map/all_to_all | solution.py:219
  122.8 5.0 %collective-permute-done.3.ext_ref = bf16[15,128,256]{2,1,0:T(8,128)(2,1)} collective-permute-done((bf16[15,128,256]{2,1,0:T(8,128)(2,1)}, bf16[15,128,256]{2,1,0:T(8,128)(2,1)}, u32[]{:S(2)}, u32[]{:S(2)}) %collective-permute-start.3) | collective-permute-done | bytes 983072 | tf_op jit(solution)/shard_map/ppermute | solution.py:210
  127.8 9.6 %shard_map.59 = f32[8,15,16,256]{3,2,1,0:T(8,128)S(1)} custom-call(f32[15,128,256]{2,1,0:T(8,128)S(1)} %copy-done.9, bf16[15,128,256]{2,1,0:T(8,128)(2,1)} %collective-permute-done.3.ext_ref, f32[8,256]{1,0:T(8,128)S(1)} %slice_bitcast_fusion.1._, f32[120,128]{1,0:T(8,128)S(1)} %copy-done.29, f32[16,256]{1,0:T(8,128)S(1)} %copy-done.12, ...), custom_call_target="tpu_custom_call" | custom-call | flops 1000 | bytes 1000 | tf_op jit(solution)/shard_map/pallas_call | solution.py:23
  146.1 11.7 %all-to-all-done.1 = f16[8,15,16,256]{3,2,1,0:T(8,128)(2,1)S(1)} async-done(((f16[8,15,16,256]{3,2,1,0:T(8,128)(2,1)}), f16[8,15,16,256]{3,2,1,0:T(8,128)(2,1)S(1)}, u32[]{:S(2)}, u32[]{:S(2)}) %all-to-all-start.1) | async-done | bytes 983072 | tf_op jit(solution)/shard_map/all_to_all | solution.py:219
  161.9 6.4 %collective-permute-done.5 = bf16[15,16,256]{2,1,0:T(8,128)(2,1)S(1)} collective-permute-done((bf16[15,16,256]{2,1,0:T(8,128)(2,1)S(1)}, bf16[15,16,256]{2,1,0:T(8,128)(2,1)S(1)}, u32[]{:S(2)}, u32[]{:S(2)}) %collective-permute-start.5) | collective-permute-done | bytes 122912 | tf_op jit(solution)/shard_map/ppermute | solution.py:210
  172.9 27.0 %all_to_all.35.refs_0_ = bf16[8,32,16,256]{3,2,1,0:T(8,128)(2,1)S(1)} all-to-all(bf16[8,32,16,256]{3,2,1,0:T(8,128)(2,1)S(1)} %fusion), channel_id=1, replica_groups=mesh['view'=8,'gz'=32] {'view'}, dimensions={0} | all-to-all | bytes 4194304 | tf_op jit(solution)/shard_map/all_to_all | solution.py:219
  199.8 7.6 %shard_map.60 = (f32[17,128,256]{2,1,0:T(8,128)S(1)}, bf16[17,128,256]{2,1,0:T(8,128)(2,1)S(1)}) custom-call(bf16[8,32,16,256]{3,2,1,0:T(8,128)(2,1)S(1)} %all_to_all.35.refs_0_, f32[16,256]{1,0:T(8,128)S(1)} %copy-done.12, bf16[17,128,256]{2,1,0:T(8,128)(2,1)S(1)} %dynamic-slice_bitcast_fusion.recorded_ref.refs_2_, f32[128,128]{1,0:T(8,128)S(1)} %copy-done.15, ...), custom_call_target="tpu_custom_call" | custom-call | flops 1000 | bytes 1000 | tf_op jit(solution)/shard_map/pallas_call | solution.py:23
  207.6 6.7 %shard_map.61 = (f32[15,128,256]{2,1,0:T(8,128)S(1)}, bf16[15,128,256]{2,1,0:T(8,128)(2,1)S(1)}) custom-call(bf16[8,32,16,256]{3,2,1,0:T(8,128)(2,1)S(1)} %all_to_all.35.refs_0_, f32[16,256]{1,0:T(8,128)S(1)} %copy-done.12, bf16[15,128,256]{2,1,0:T(8,128)(2,1)S(1)} %copy-done.4, f32[128,128]{1,0:T(8,128)S(1)} %copy-done.15, f32[256,256]{1,0:T(8,128)S(1)} %copy-done.7, ...), custom_call_target="tpu_custom_call" | custom-call | flops 1000 | bytes 1000 | tf_op jit(solution)/shard_map/pallas_call | solution.py:23
  215.2 11.5 %shard_map.62 = (f32[8,17,16,256]{3,2,1,0:T(8,128)S(1)}, f32[15,128,256]{2,1,0:T(8,128)S(1)}) custom-call(f32[17,128,256]{2,1,0:T(8,128)S(1)} %get-tuple-element.45.far_q_ref, f32[15,128,256]{2,1,0:T(8,128)S(1)} %get-tuple-element.46.near_q_ref, bf16[17,128,256]{2,1,0:T(8,128)(2,1)S(1)} %collective-permute-done.6.sib_ref, f32[256,256]{1,0:T(8,128)S(1)} %copy-done.18, ...), custom_call_target="tpu_custom_call" | custom-call | flops 1000 | bytes 1000 | tf_op jit(solution)/shard_map/pallas_call | solution.py:23
  233.7 5.1 %collective-permute-start.7 = (bf16[15,128,256]{2,1,0:T(8,128)(2,1)}, bf16[15,128,256]{2,1,0:T(8,128)(2,1)S(1)}, u32[]{:S(2)}, u32[]{:S(2)}) collective-permute-start(bf16[15,128,256]{2,1,0:T(8,128)(2,1)} %copy-done.34), channel_id=1, source_target_pairs={{1,2},{3,4},{5,6},{7,8},{9,10},{11,12},{13,14},{15,16},{17,18},{19... | collective-permute-start | bytes 2949128 | tf_op jit(solution)/shard_map/ppermute | solution.py:210
  238.8 22.8 %all-to-all-done.4 = f16[8,17,16,256]{3,2,1,0:T(8,128)(2,1)} async-done(((f16[8,17,16,256]{3,2,1,0:T(8,128)(2,1)}), f16[8,17,16,256]{3,2,1,0:T(8,128)(2,1)}, u32[]{:S(2)}, u32[]{:S(2)}) %all-to-all-start.4) | async-done | bytes 1114144 | tf_op jit(solution)/shard_map/all_to_all | solution.py:219
  263.1 8.3 %collective-permute-done.7.ext_ref = bf16[15,128,256]{2,1,0:T(8,128)(2,1)S(1)} collective-permute-done((bf16[15,128,256]{2,1,0:T(8,128)(2,1)}, bf16[15,128,256]{2,1,0:T(8,128)(2,1)S(1)}, u32[]{:S(2)}, u32[]{:S(2)}) %collective-permute-start.7) | collective-permute-done | bytes 983072 | tf_op jit(solution)/shard_map/ppermute | solution.py:210
  271.4 8.4 %shard_map.63 = f32[8,15,16,256]{3,2,1,0:T(8,128)S(1)} custom-call(f32[15,128,256]{2,1,0:T(8,128)S(1)} %copy-done.11, bf16[15,128,256]{2,1,0:T(8,128)(2,1)S(1)} %collective-permute-done.7.ext_ref, f32[8,256]{1,0:T(8,128)S(1)} %slice_bitcast_fusion._, f32[120,128]{1,0:T(8,128)S(1)} %copy-done.29, f32[16,256]{1,0:T(8,128)S(1)} %copy-done.12, ...), custom_call_target="tpu_custom_call" | custom-call | flops 1000 | bytes 1000 | tf_op jit(solution)/shard_map/pallas_call | solution.py:23
  285.6 15.3 %all-to-all-done.5 = f16[8,15,16,256]{3,2,1,0:T(8,128)(2,1)S(1)} async-done(((f16[8,15,16,256]{3,2,1,0:T(8,128)(2,1)}), f16[8,15,16,256]{3,2,1,0:T(8,128)(2,1)S(1)}, u32[]{:S(2)}, u32[]{:S(2)}) %all-to-all-start.5) | async-done | bytes 983072 | tf_op jit(solution)/shard_map/all_to_all | solution.py:219
  302.0 31.3 %all_to_all.36 = f16[8,34,16,256]{3,2,1,0:T(8,128)(2,1)S(1)} all-to-all(f16[8,34,16,256]{3,2,1,0:T(8,128)(2,1)S(1)} %broadcast_in_dim.8), channel_id=1, replica_groups=mesh['view'=8,'gz'=32] {'view'}, dimensions={0} | all-to-all | bytes 4456448 | tf_op jit(solution)/shard_map/all_to_all | solution.py:219
  (150 shorter events, 57.1 us)
Async XLA Ops:
  0.0 14.9 %copy-start = (bf16[1,32,128,256]{3,2,1,0:T(8,128)(2,1)S(1)}, bf16[1,32,128,256]{3,2,1,0:T(8,128)(2,1)}, u32[]{:S(2)}) copy-start(bf16[1,32,128,256]{3,2,1,0:T(8,128)(2,1)} %param.5) | copy-start | bytes 6291460
  0.0 15.1 %copy-start.12 = (f32[16,256]{1,0:T(8,128)S(1)}, f32[16,256]{1,0:T(8,128)}, u32[]{:S(2)}) copy-start(f32[16,256]{1,0:T(8,128)} %constant.101.clone.unspread_ref.refs_1_) | copy-start | bytes 49156
  3.0 12.0 %collective-permute-start = (bf16[17,128,256]{2,1,0:T(8,128)(2,1)}, bf16[17,128,256]{2,1,0:T(8,128)(2,1)}, u32[]{:S(2)}, u32[]{:S(2)}) collective-permute-start(bf16[17,128,256]{2,1,0:T(8,128)(2,1)} %multiply_convert_fusion), channel_id=1, source_target_pairs={{0,1},{1,0},{2,3},{3,2},{4,5},{5,4},{6,7},{7,6},{8,9},{9,8},{10,11... | collective-permute-start | bytes 3342344 | tf_op jit(solution)/shard_map/ppermute | solution.py:215
  31.8 30.7 %copy-start.31 = (f32[120,128]{1,0:T(8,128)S(1)}, f32[120,128]{1,0:T(8,128)}, u32[]{:S(2)}) copy-start(f32[120,128]{1,0:T(8,128)} %copy-done.30) | copy-start | bytes 184324
  31.8 39.1 %collective-permute-start.2 = (bf16[17,128,256]{2,1,0:T(8,128)(2,1)S(1)}, bf16[17,128,256]{2,1,0:T(8,128)(2,1)S(1)}, u32[]{:S(2)}, u32[]{:S(2)}) collective-permute-start(bf16[17,128,256]{2,1,0:T(8,128)(2,1)S(1)} %get-tuple-element.36), channel_id=1, source_target_pairs={{0,1},{1,0},{2,3},{3,2},{4,5},{5,4},{6,7},{7,6},{8,9},{9,8},{10,11... | collective-permute-start | bytes 3342344 | tf_op jit(solution)/shard_map/ppermute | solution.py:215
  32.6 29.9 %collective-permute-start.1 = (bf16[15,128,256]{2,1,0:T(8,128)(2,1)S(1)}, bf16[15,128,256]{2,1,0:T(8,128)(2,1)S(1)}, u32[]{:S(2)}, u32[]{:S(2)}) collective-permute-start(bf16[15,128,256]{2,1,0:T(8,128)(2,1)S(1)} %multiply_convert_fusion.1), channel_id=1, source_target_pairs={{1,2},{3,4},{5,6},{7,8},{9,10},{11,12},{13,14},{15,16},{17,18},{19... | collective-permute-start | bytes 2949128 | tf_op jit(solution)/shard_map/ppermute | solution.py:210
  40.5 30.5 %copy-start.3 = (bf16[15,128,256]{2,1,0:T(8,128)(2,1)}, bf16[15,128,256]{2,1,0:T(8,128)(2,1)S(1)}, u32[]{:S(2)}) copy-start(bf16[15,128,256]{2,1,0:T(8,128)(2,1)S(1)} %dynamic-slice_bitcast_fusion.1.recorded_ref.refs_2_) | copy-start | bytes 2949124
  85.1 42.7 %copy-start.9 = (f32[15,128,256]{2,1,0:T(8,128)S(1)}, f32[15,128,256]{2,1,0:T(8,128)}, u32[]{:S(2)}) copy-start(f32[15,128,256]{2,1,0:T(8,128)} %copy-done.8) | copy-start | bytes 5898244
  85.1 42.7 %copy-start.29 = (f32[120,128]{1,0:T(8,128)S(1)}, f32[120,128]{1,0:T(8,128)}, u32[]{:S(2)}) copy-start(f32[120,128]{1,0:T(8,128)} %copy-done.28) | copy-start | bytes 184324
  85.1 29.6 %all-to-all-start = ((f16[8,17,16,256]{3,2,1,0:T(8,128)(2,1)}), f16[8,17,16,256]{3,2,1,0:T(8,128)(2,1)}, u32[]{:S(2)}, u32[]{:S(2)}) async-start(f16[8,17,16,256]{3,2,1,0:T(8,128)(2,1)} %convert_element_type.64), calls=%async_computation | async-start | bytes 2228224 | tf_op jit(solution)/shard_map/all_to_all | solution.py:219
  90.1 37.7 %collective-permute-start.3 = (bf16[15,128,256]{2,1,0:T(8,128)(2,1)}, bf16[15,128,256]{2,1,0:T(8,128)(2,1)}, u32[]{:S(2)}, u32[]{:S(2)}) collective-permute-start(bf16[15,128,256]{2,1,0:T(8,128)(2,1)} %copy-done.33), channel_id=1, source_target_pairs={{1,2},{3,4},{5,6},{7,8},{9,10},{11,12},{13,14},{15,16},{17,18},{19... | collective-permute-start | bytes 2949128 | tf_op jit(solution)/shard_map/ppermute | solution.py:210
  115.3 23.3 %all-to-all-start.2 = ((f32[8,8,128]{2,1,0:T(8,128)}), f32[8,8,128]{2,1,0:T(8,128)S(1)}, u32[]{:S(2)}, u32[]{:S(2)}) async-start(f32[8,8,128]{2,1,0:T(8,128)} %broadcast_in_dim.6), calls=%async_computation.2 | async-start | bytes 65536 | tf_op jit(solution)/shard_map/all_to_all | solution.py:219
  138.6 19.2 %all-to-all-start.1 = ((f16[8,15,16,256]{3,2,1,0:T(8,128)(2,1)}), f16[8,15,16,256]{3,2,1,0:T(8,128)(2,1)S(1)}, u32[]{:S(2)}, u32[]{:S(2)}) async-start(f16[8,15,16,256]{3,2,1,0:T(8,128)(2,1)} %convert_element_type.66), calls=%async_computation.1 | async-start | bytes 1966080 | tf_op jit(solution)/shard_map/all_to_all | solution.py:219
  146.1 22.4 %copy-start.35 = (f32[17,16,256]{2,1,0:T(8,128)}, f32[17,16,256]{2,1,0:T(8,128)S(1)}, u32[]{:S(2)}) copy-start(f32[17,16,256]{2,1,0:T(8,128)S(1)} %get-tuple-element.54) | copy-start | bytes 835588
  146.1 14.9 %collective-permute-start.4 = (bf16[17,16,256]{2,1,0:T(8,128)(2,1)}, bf16[17,16,256]{2,1,0:T(8,128)(2,1)}, u32[]{:S(2)}, u32[]{:S(2)}) collective-permute-start(bf16[17,16,256]{2,1,0:T(8,128)(2,1)} %get-tuple-element.53), channel_id=1, source_target_pairs={{0,1},{1,0},{2,3},{3,2},{4,5},{5,4},{6,7},{7,6},{8,9},{9,8},{10,11... | collective-permute-start | bytes 417800 | tf_op jit(solution)/shard_map/ppermute | solution.py:215
  159.1 9.3 %collective-permute-start.5 = (bf16[15,16,256]{2,1,0:T(8,128)(2,1)S(1)}, bf16[15,16,256]{2,1,0:T(8,128)(2,1)S(1)}, u32[]{:S(2)}, u32[]{:S(2)}) collective-permute-start(bf16[15,16,256]{2,1,0:T(8,128)(2,1)S(1)} %get-tuple-element.55), channel_id=1, source_target_pairs={{1,2},{3,4},{5,6},{7,8},{9,10},{11,12},{13,14},{15,16},{17,18},{19... | collective-permute-start | bytes 368648 | tf_op jit(solution)/shard_map/ppermute | solution.py:210
  172.9 27.0 %copy-start.7 = (f32[256,256]{1,0:T(8,128)S(1)}, f32[256,256]{1,0:T(8,128)}, u32[]{:S(2)}) copy-start(f32[256,256]{1,0:T(8,128)} %copy-done.5) | copy-start | bytes 786436
  172.9 27.0 %copy-start.15 = (f32[128,128]{1,0:T(8,128)S(1)}, f32[128,128]{1,0:T(8,128)}, u32[]{:S(2)}) copy-start(f32[128,128]{1,0:T(8,128)} %copy-done.13) | copy-start | bytes 196612
  207.4 7.8 %collective-permute-start.6 = (bf16[17,128,256]{2,1,0:T(8,128)(2,1)S(1)}, bf16[17,128,256]{2,1,0:T(8,128)(2,1)S(1)}, u32[]{:S(2)}, u32[]{:S(2)}) collective-permute-start(bf16[17,128,256]{2,1,0:T(8,128)(2,1)S(1)} %get-tuple-element.47), channel_id=1, source_target_pairs={{0,1},{1,0},{2,3},{3,2},{4,5},{5,4},{6,7},{7,6},{8,9},{9,8},{10,11... | collective-permute-start | bytes 3342344 | tf_op jit(solution)/shard_map/ppermute | solution.py:215
  229.3 42.1 %copy-start.11 = (f32[15,128,256]{2,1,0:T(8,128)S(1)}, f32[15,128,256]{2,1,0:T(8,128)}, u32[]{:S(2)}) copy-start(f32[15,128,256]{2,1,0:T(8,128)} %copy-done.10) | copy-start | bytes 5898244
  229.3 32.3 %all-to-all-start.4 = ((f16[8,17,16,256]{3,2,1,0:T(8,128)(2,1)}), f16[8,17,16,256]{3,2,1,0:T(8,128)(2,1)}, u32[]{:S(2)}, u32[]{:S(2)}) async-start(f16[8,17,16,256]{3,2,1,0:T(8,128)(2,1)} %convert_element_type.74), calls=%async_computation.4 | async-start | bytes 2228224 | tf_op jit(solution)/shard_map/all_to_all | solution.py:219
  233.7 37.7 %collective-permute-start.7 = (bf16[15,128,256]{2,1,0:T(8,128)(2,1)}, bf16[15,128,256]{2,1,0:T(8,128)(2,1)S(1)}, u32[]{:S(2)}, u32[]{:S(2)}) collective-permute-start(bf16[15,128,256]{2,1,0:T(8,128)(2,1)} %copy-done.34), channel_id=1, source_target_pairs={{1,2},{3,4},{5,6},{7,8},{9,10},{11,12},{13,14},{15,16},{17,18},{19... | collective-permute-start | bytes 2949128 | tf_op jit(solution)/shard_map/ppermute | solution.py:210
  281.0 20.0 %copy-start.38 = (f32[15,16,256]{2,1,0:T(8,128)S(1)}, f32[15,16,256]{2,1,0:T(8,128)}, u32[]{:S(2)}) copy-start(f32[15,16,256]{2,1,0:T(8,128)} %copy-done.37) | copy-start | bytes 737284
  281.0 19.9 %all-to-all-start.5 = ((f16[8,15,16,256]{3,2,1,0:T(8,128)(2,1)}), f16[8,15,16,256]{3,2,1,0:T(8,128)(2,1)S(1)}, u32[]{:S(2)}, u32[]{:S(2)}) async-start(f16[8,15,16,256]{3,2,1,0:T(8,128)(2,1)} %convert_element_type.76), calls=%async_computation.5 | async-start | bytes 1966080 | tf_op jit(solution)/shard_map/all_to_all | solution.py:219
  (34 other events, 136.2 us)
